TPU v7x, 32 devices: a whole 2x2x4 slice. The times are simulated.
32 devices in a mesh: layer: 4 (over z), row: 4 (over y, x), col: 2 (over core).
Axes of the slice: x: 2, y: 2, z: 4, core: 2. Of those that a mesh axis runs over, the one named last changes fastest.
Arguments:
- leaf_rhs: float32 [4, 3, 1024, 256], P('layer', None, 'row'), may hold values from -6 to 6
- anc_rhs: float32 [2, 1024, 256], P(None, 'row'), may hold values from -6 to 6
- leaf_tiles: bfloat16 [4, 3, 1024, 1024], P('layer', None, 'row', 'col'), may hold values from -0.1875 to 0.1875
- cross_tiles: bfloat16 [4, 2, 3, 1024, 1024], P('layer', None, None, 'row', 'col'), may hold values from -0.09375 to 0.09375
- top_tiles: bfloat16 [1, 1024, 1024], P(None, 'row', 'col'), may hold values from -0.1875 to 0.1875
- leaf_pattern: int32 [4, 3, 8, 8], P('layer', None, 'row', 'col'), may hold values 0 or 1
- cross_pattern: int32 [4, 2, 3, 8, 8], P('layer', None, None, 'row', 'col'), may hold values 0 or 1
- top_pattern: int32 [1, 8, 8], P(None, 'row', 'col'), may hold values 0 or 1
- leaf_inverse: bfloat16 [4, 3, 8, 128, 128], P('layer'), may hold values from -0.5 to 0.5
- anc_inverse: bfloat16 [2, 8, 128, 128], replicated, may hold values from -0.5 to 0.5
Outputs:
- leaf_solution: bfloat16 [4, 3, 1024, 256], P('layer', None, 'row')
- anc_solution: bfloat16 [2, 1024, 256], P(None, 'row')
All inputs are finite; a program needn't handle non-finite values. No bound on the sum of `leaf_pattern` or of `cross_pattern` or of `top_pattern` on one device may be relied on, other than what follows from the above.
Results may differ from a plain program's by a relative error of at most 0.023.
Values may be sent and summed in bfloat16 or wider, within the bound.
A program may use at most 128 MiB of HBM per device.

v0:
```python
import jax
import jax.numpy as jnp
from jax import lax
from jax.sharding import PartitionSpec as P


def pair_index(target, source):
    return target * (target - 1) // 2 + source


def expand_mask(pattern, tiles, tile_width):
    grown = jnp.repeat(jnp.repeat(pattern, tile_width, axis=-2), tile_width, axis=-1)
    return tiles * grown.astype(tiles.dtype)


def forward_product(masked, vector):
    return jnp.dot(masked, vector, preferred_element_type=jnp.float32)


def backward_product(masked, vector):
    return lax.dot_general(
        masked, vector, (((0,), (0,)), ((), ())), preferred_element_type=jnp.float32
    )


def solve_blocks(inverse, first_block, residual, flipped):
    tile_width = inverse.shape[-1]
    number = residual.shape[0] // tile_width
    blocks = lax.dynamic_slice_in_dim(inverse, first_block, number, 0)
    pieces = residual.astype(jnp.bfloat16).reshape(number, tile_width, residual.shape[1])
    text_form = "sji,sjk->sik" if flipped else "sij,sjk->sik"
    solved = jnp.einsum(text_form, blocks, pieces, preferred_element_type=jnp.float32)
    return solved.reshape(residual.shape).astype(jnp.bfloat16)


def local(
    leaf_rhs,
    anc_rhs,
    leaf_tiles,
    cross_tiles,
    top_tiles,
    leaf_pattern,
    cross_pattern,
    top_pattern,
    leaf_inverse,
    anc_inverse,
):
    tile_width = leaf_inverse.shape[-1]
    row_count = leaf_rhs.shape[2]
    col_count = leaf_tiles.shape[3]
    leaf_levels = leaf_rhs.shape[1]
    anc_levels = anc_rhs.shape[0]
    col_devices = lax.axis_size("col")
    row_index = lax.axis_index("row")
    col_index = lax.axis_index("col")
    row_first = row_index * (row_count // tile_width)
    col_first = col_index * (col_count // tile_width)
    leaf_masked = expand_mask(leaf_pattern[0], leaf_tiles[0], tile_width)
    cross_masked = expand_mask(cross_pattern[0], cross_tiles[0], tile_width)
    top_masked = expand_mask(top_pattern, top_tiles, tile_width)
    leaf_blocks = leaf_inverse[0]
    leaf_columns = []
    for target in range(leaf_levels):
        rhs_rows = leaf_rhs[0, target]
        partial_value = None
        for source in range(target):
            term_now = forward_product(
                leaf_masked[pair_index(target, source)], leaf_columns[source]
            )
            partial_value = term_now if partial_value is None else partial_value + term_now
        share_rows = row_count // col_devices
        own_rhs = lax.dynamic_slice_in_dim(rhs_rows, col_index * share_rows, share_rows, 0)
        if partial_value is None:
            residual = own_rhs
        else:
            residual = own_rhs - lax.psum_scatter(
                partial_value.astype(jnp.bfloat16), "col", scatter_dimension=0, tiled=True
            ).astype(jnp.float32)
        solved = solve_blocks(
            leaf_blocks[target], row_first + col_index * (share_rows // tile_width), residual, False
        )
        row_block = lax.all_gather(solved, "col", axis=0, tiled=True)
        whole = lax.all_gather(row_block, "row", axis=0, tiled=True)
        column_part = lax.dynamic_slice_in_dim(whole, col_index * col_count, col_count, 0)
        leaf_columns.append(column_part)
    leaf_terms = []
    for target in range(anc_levels):
        term_sum = forward_product(cross_masked[target, 0], leaf_columns[0])
        for source in range(1, leaf_levels):
            term_sum = term_sum + forward_product(
                cross_masked[target, source], leaf_columns[source]
            )
        leaf_terms.append(term_sum)
    lower_sums = lax.psum(jnp.stack(leaf_terms).astype(jnp.bfloat16), ("layer", "col")).astype(
        jnp.float32
    )
    anc_rows = []
    anc_columns = []
    for target in range(anc_levels):
        upper_part = None
        for source in range(target):
            term_now = forward_product(top_masked[pair_index(target, source)], anc_columns[source])
            upper_part = term_now
        summed = lower_sums[target]
        if upper_part is not None:
            summed = summed + lax.psum(upper_part.astype(jnp.bfloat16), "col").astype(jnp.float32)
        solved = solve_blocks(anc_inverse[target], row_first, anc_rhs[target] - summed, False)
        anc_rows.append(solved)
        whole = lax.all_gather(solved, "row", axis=0, tiled=True)
        anc_columns.append(lax.dynamic_slice_in_dim(whole, col_index * col_count, col_count, 0))

    def finish(partial_value, column_values, inverse):
        summed = lax.psum(partial_value.astype(jnp.bfloat16), "row").astype(jnp.float32)
        residual = column_values.astype(jnp.float32) - summed
        solved = solve_blocks(inverse, col_first, residual, True)
        whole = lax.all_gather(solved, "col", axis=0, tiled=True)
        return lax.dynamic_slice_in_dim(whole, row_index * row_count, row_count, 0)

    anc_out = [None] * anc_levels
    anc_out[anc_levels - 1] = solve_blocks(
        anc_inverse[anc_levels - 1], row_first, anc_rows[anc_levels - 1], True
    )
    target = 0
    partial_value = backward_product(
        top_masked[pair_index(target + 1, target)], anc_out[target + 1]
    )
    anc_out[target] = finish(partial_value, anc_columns[target], anc_inverse[target])
    leaf_out = [None] * leaf_levels
    for target in range(leaf_levels - 1, -1, -1):
        partial_value = backward_product(cross_masked[0, target], anc_out[0])
        partial_value = partial_value + backward_product(cross_masked[1, target], anc_out[1])
        for source in range(target + 1, leaf_levels):
            partial_value = partial_value + backward_product(
                leaf_masked[pair_index(source, target)], leaf_out[source]
            )
        leaf_out[target] = finish(partial_value, leaf_columns[target], leaf_blocks[target])
    return (jnp.stack(leaf_out)[None], jnp.stack(anc_out))


def solution(mesh):
    in_specs = (
        P("layer", None, "row", None),
        P(None, "row", None),
        P("layer", None, "row", "col"),
        P("layer", None, None, "row", "col"),
        P(None, "row", "col"),
        P("layer", None, "row", "col"),
        P("layer", None, None, "row", "col"),
        P(None, "row", "col"),
        P("layer", None, None, None, None),
        P(),
    )
    out_specs = (P("layer", None, "row", None), P(None, "row", None))
    return jax.shard_map(local, mesh=mesh, in_specs=in_specs, out_specs=out_specs, check_vma=False)
```

profile of v0, /device:TPU:0, one launch (start us, length us, event | category | flops | bytes accessed | tf_op | source)
XLA Modules:
  0.0 374.0 jit_solution(7941066269965854407)
XLA Ops:
  8.2 2.0 fusion.90
  10.9 2.0 all_gather.33
  12.9 11.5 %all_gather.34 = bf16[1024,256]{1,0:T(8,128)(2,1)S(1)} all-gather(bf16[256,256]{1,0:T(8,128)(2,1)S(1)} %all_gather.33), channel_id=1, replica_groups=mesh['layer'=4,'row'=4,'col'=2] {'row'}, dimensions={0}, use_global_device_ids=true | all-gather | bytes 655360 | tf_op jit(solution)/shard_map/all_gather | solution.py:83
  27.8 2.0 broadcast_in_dim.22
  29.8 2.0 convert_element_type.213
  31.8 2.1 bitcast_multiply_fusion
  41.6 10.0 %all_gather.36 = bf16[1024,256]{1,0:T(8,128)(2,1)S(1)} all-gather(bf16[256,256]{1,0:T(8,128)(2,1)S(1)} %all_gather.35), channel_id=1, replica_groups=mesh['layer'=4,'row'=4,'col'=2] {'row'}, dimensions={0}, use_global_device_ids=true | all-gather | bytes 655360 | tf_op jit(solution)/shard_map/all_gather | solution.py:83
  57.3 4.1 %reduce-scatter.5.cloned.1.call-done = bf16[128,256]{1,0:T(8,128)(2,1)} async-done(((bf16[256,256]{1,0:T(8,128)(2,1)}), bf16[128,256]{1,0:T(8,128)(2,1)}) %reduce-scatter.5.cloned.1.call-update) | async-done | bytes 65552 | tf_op jit(solution)/shard_map/reduce_scatter | solution.py:76
  64.5 10.5 %all_gather.38 = bf16[1024,256]{1,0:T(8,128)(2,1)S(1)} all-gather(bf16[256,256]{1,0:T(8,128)(2,1)S(1)} %all_gather.37), channel_id=1, replica_groups=mesh['layer'=4,'row'=4,'col'=2] {'row'}, dimensions={0}, use_global_device_ids=true | all-gather | bytes 655360 | tf_op jit(solution)/shard_map/all_gather | solution.py:83
  79.3 53.1 %all-reduce.7.cloned.1.call-done = bf16[2,256,256]{2,1,0:T(8,128)(2,1)} async-done(((bf16[2,256,256]{2,1,0:T(8,128)(2,1)}), bf16[2,256,256]{2,1,0:T(8,128)(2,1)}) %all-reduce.7.cloned.1.call-update) | async-done | bytes 262160 | tf_op jit(solution)/shard_map/psum | solution.py:94
  136.3 10.7 %all_gather.39 = bf16[1024,256]{1,0:T(8,128)(2,1)S(1)} all-gather(bf16[256,256]{1,0:T(8,128)(2,1)S(1)} %bitcast.163), channel_id=1, replica_groups=mesh['layer'=4,'row'=4,'col'=2] {'row'}, dimensions={0}, use_global_device_ids=true | all-gather | bytes 655360 | tf_op jit(solution)/shard_map/all_gather | solution.py:109
  148.8 16.0 %all-reduce.9.cloned.1.call-done = bf16[256,256]{1,0:T(8,128)(2,1)} async-done(((bf16[256,256]{1,0:T(8,128)(2,1)}), bf16[256,256]{1,0:T(8,128)(2,1)}) %all-reduce.9.cloned.1.call-update) | async-done | bytes 131088 | tf_op jit(solution)/shard_map/psum | solution.py:106
  167.9 2.0 convolution_convert_fusion.4
  170.0 44.2 %all-reduce.11.cloned.1.call-done = bf16[512,256]{1,0:T(8,128)(2,1)} async-done(((bf16[512,256]{1,0:T(8,128)(2,1)}), bf16[512,256]{1,0:T(8,128)(2,1)}) %all-reduce.11.cloned.1.call-update) | async-done | bytes 262160 | tf_op jit(solution)/shard_map/psum | solution.py:113
  216.5 2.2 all_gather.40
  221.6 2.0 fusion.14
  223.6 2.1 convolution_add_fusion.4
  225.8 38.9 %all-reduce.13.cloned.1.call-done = bf16[512,256]{1,0:T(8,128)(2,1)} async-done(((bf16[512,256]{1,0:T(8,128)(2,1)}), bf16[512,256]{1,0:T(8,128)(2,1)}) %all-reduce.13.cloned.1.call-update) | async-done | bytes 262160 | tf_op jit(solution)/shard_map/psum | solution.py:113
  267.0 2.2 all_gather.41
  272.6 2.1 convolution_add_fusion.5
  274.7 39.3 %all-reduce.15.cloned.1.call-done = bf16[512,256]{1,0:T(8,128)(2,1)} async-done(((bf16[512,256]{1,0:T(8,128)(2,1)}), bf16[512,256]{1,0:T(8,128)(2,1)}) %all-reduce.15.cloned.1.call-update) | async-done | bytes 262160 | tf_op jit(solution)/shard_map/psum | solution.py:113
  316.3 2.2 all_gather.42
  321.5 41.4 %all-reduce.17.cloned.1.call-done = bf16[512,256]{1,0:T(8,128)(2,1)} async-done(((bf16[512,256]{1,0:T(8,128)(2,1)}), bf16[512,256]{1,0:T(8,128)(2,1)}) %all-reduce.17.cloned.1.call-update) | async-done | bytes 262160 | tf_op jit(solution)/shard_map/psum | solution.py:113
  364.2 2.2 all_gather.43
  (106 shorter events, 52.7 us)
Async XLA Ops:
  7.2 17.2 %copy-start.15 = (s32[1,3,2,4]{3,2,1,0:T(2,128)S(1)}, s32[1,3,2,4]{3,2,1,0:T(2,128)}, u32[]{:S(2)}) copy-start(s32[1,3,2,4]{3,2,1,0:T(2,128)} %param.15) | copy-start | bytes 292
  7.2 31.5 %reduce-scatter.3.cloned.1.call-start = ((), (), s32[]{:S(2)}) async-start(), calls=%async_computation.2 | async-start | bytes 196608 | tf_op jit(solution)/shard_map/reduce_scatter | solution.py:76
  12.9 12.9 %copy-start.11 = (bf16[1,3,256,512]{3,2,1,0:T(8,128)(2,1)S(1)}, bf16[1,3,256,512]{3,2,1,0:T(8,128)(2,1)}, u32[]{:S(2)}) copy-start(bf16[1,3,256,512]{3,2,1,0:T(8,128)(2,1)} %param.12) | copy-start | bytes 2359300
  25.7 2.0 copy-start.14
  26.8 34.7 %reduce-scatter.5.cloned.1.call-start = ((), (), s32[]{:S(2)}) async-start(), calls=%async_computation.3 | async-start | bytes 196608 | tf_op jit(solution)/shard_map/reduce_scatter | solution.py:76
  33.9 1.9 copy-start.16
  53.5 78.9 %all-reduce.7.cloned.1.call-start = ((), (), s32[]{:S(2)}) async-start(), calls=%async_computation.4 | async-start | bytes 524288 | tf_op jit(solution)/shard_map/psum | solution.py:94
  61.4 14.9 %copy-start.10 = (f32[256,256]{1,0:T(8,128)S(1)}, f32[256,256]{1,0:T(8,128)}, u32[]{:S(2)}) copy-start(f32[256,256]{1,0:T(8,128)} %convolution_add_fusion.10) | copy-start | bytes 786436
  75.0 1.4 copy-start
  77.3 87.5 %all-reduce.9.cloned.1.call-start = ((), (), s32[]{:S(2)}) async-start(), calls=%async_computation.5 | async-start | bytes 262144 | tf_op jit(solution)/shard_map/psum | solution.py:106
  132.4 15.4 %copy-start.1 = (bf16[1,256,512]{2,1,0:T(8,128)(2,1)S(1)}, bf16[1,256,512]{2,1,0:T(8,128)(2,1)}, u32[]{:S(2)}) copy-start(bf16[1,256,512]{2,1,0:T(8,128)(2,1)} %convert_element_type.235) | copy-start | bytes 786436
  132.4 15.4 %copy-start.9 = (bf16[1,256,512]{2,1,0:T(8,128)(2,1)S(1)}, bf16[1,256,512]{2,1,0:T(8,128)(2,1)}, u32[]{:S(2)}) copy-start(bf16[1,256,512]{2,1,0:T(8,128)(2,1)} %param.14) | copy-start | bytes 786436
  133.5 0.8 copy-start.3
  147.0 0.8 copy-start.4
  148.7 65.5 %all-reduce.11.cloned.1.call-start = ((), (), s32[]{:S(2)}) async-start(), calls=%async_computation.6 | async-start | bytes 524288 | tf_op jit(solution)/shard_map/psum | solution.py:113
  170.0 94.7 %all-reduce.13.cloned.1.call-start = ((), (), s32[]{:S(2)}) async-start(), calls=%async_computation.7 | async-start | bytes 524288 | tf_op jit(solution)/shard_map/psum | solution.py:113
  218.7 0.8 copy-start.2
  221.6 92.5 %all-reduce.15.cloned.1.call-start = ((), (), s32[]{:S(2)}) async-start(), calls=%async_computation.8 | async-start | bytes 524288 | tf_op jit(solution)/shard_map/psum | solution.py:113
  264.7 5.3 %copy-start.6 = (f32[512,256]{1,0:T(8,128)S(1)}, f32[512,256]{1,0:T(8,128)}, u32[]{:S(2)}) copy-start(f32[512,256]{1,0:T(8,128)} %convolution_add_fusion.4) | copy-start | bytes 1572868
  269.2 0.8 copy-start.7
  271.0 91.9 %all-reduce.17.cloned.1.call-start = ((), (), s32[]{:S(2)}) async-start(), calls=%async_computation.9 | async-start | bytes 524288 | tf_op jit(solution)/shard_map/psum | solution.py:113
  274.7 43.8 %copy-start.5 = (f32[512,256]{1,0:T(8,128)S(1)}, f32[512,256]{1,0:T(8,128)}, u32[]{:S(2)}) copy-start(f32[512,256]{1,0:T(8,128)} %convolution_add_fusion.5) | copy-start | bytes 1572868
  315.1 3.7 copy-start.8
  318.8 45.1 %copy-start.13 = (bf16[1,1,8,128,128]{4,3,2,1,0:T(8,128)(2,1)S(1)}, bf16[1,1,8,128,128]{4,3,2,1,0:T(8,128)(2,1)}, u32[]{:S(2)}) copy-start(bf16[1,1,8,128,128]{4,3,2,1,0:T(8,128)(2,1)} %copy-done.12) | copy-start | bytes 786436
  (1 other events, 0.7 us)
Sparse Core Ops, SparseCore 0:
  26.9 7.7 reduce-scatter.2
  53.6 7.7 reduce-scatter.4
  77.5 54.9 all-reduce.6
  148.8 15.9 all-reduce.8
  170.1 44.0 all-reduce.10
  221.7 42.9 all-reduce.12
  271.1 42.9 all-reduce.14
  319.9 42.9 all-reduce.16
where the time goes:
time: 375 us; the launch traced here: 374 us
  waiting for transfers between devices  237 us (63%)
  blocking collectives  57.2 us (15%)
  matrix products  33.1 us (9%)
  local copies, waits for them, and re-layouts  18.2 us (5%)
  between operations  14.5 us (4%)
  other arithmetic  13.4 us (4%)
    psum x4, waiting for transfers between devices, finish(): lax.psum(partial_value.astype(jnp.bfloat16), 'row').astype(jnp.float32)  164 us
    psum x1, waiting for transfers between devices, local(): lax.psum(jnp.stack(leaf_terms).astype(jnp.bfloat16), ('layer', 'col'))  53.1 us
    all_gather x3, blocking collectives, local(): whole = lax.all_gather(row_block, 'row', axis=0, tiled=True)  32 us
    psum x1, waiting for transfers between devices, local(): lax.psum(upper_part.astype(jnp.bfloat16), 'col').astype(jnp.float32)  16 us
    dot_general x10, matrix products, backward_product(): lax.dot_general(masked, vector, (((0,), (0,)), ((), ())), preferred_eleme...  12.8 us
    dot_general x10, matrix products, forward_product(): return jnp.dot(masked, vector, preferred_element_type=jnp.float32)  11.8 us
    all_gather x1, blocking collectives, local(): whole = lax.all_gather(solved, 'row', axis=0, tiled=True)  10.7 us
    all_gather x4, blocking collectives, finish(): whole = lax.all_gather(solved, 'col', axis=0, tiled=True)  8.73 us
  transfers between devices with their start and end apart: 8, of which 7 were waited for; matrix products, arithmetic and copies ran while one was open for 7% of the time, Pallas kernels for 0%

commit v1 on v0

v1 whole, which is shorter than its diff:
```python
import functools

import jax
import jax.numpy as jnp
from jax import lax
from jax.experimental import pallas as pl
from jax.experimental.pallas import tpu as pltpu
from jax.sharding import PartitionSpec as P

MESH = pl.DeviceIdType.MESH
NT = (((1,), (1,)), ((), ()))
NN = (((1,), (0,)), ((), ()))
F32 = jnp.float32
BF16 = jnp.bfloat16


def pair_index(target, source):
    return target * (target - 1) // 2 + source


def dot(left, right, form):
    return lax.dot_general(left, right, form, preferred_element_type=F32)


def loop(start, stop, body, init):
    if stop - start <= 4:
        carry = init
        for index in range(start, stop):
            carry = body(index, carry)
        return carry
    return lax.fori_loop(start, stop, body, init)


def solve(inverse, level, residual, flipped):
    wide = inverse.shape[-1]
    pieces = []
    rounded = residual.astype(BF16)
    for block in range(inverse.shape[1]):
        part = rounded[:, block * wide : (block + 1) * wide]
        pieces.append(dot(part, inverse[level, block], NN if flipped else NT))
    return jnp.concatenate(pieces, axis=1)


def kernel(
    dims,
    leaf_rhs, anc_rhs, leaf_tiles, cross_tiles, top_tiles,
    leaf_pat, cross_pat, top_pat, leaf_inv, anc_inv,
    leaf_out, anc_out,
    rhs_in, arhs_in, inv, ainv, rhs_t, arhs_t, leaf_m, cross_m, top_m,
    ybuf, fsum, csum, zs, zr, zbuf, xanc, asend, arecv,
    bsum, bown, bsend, brecv, xbuf, stage,
    load_sem, col_ssem, col_rsem, y_ssem, y_rsem, z_ssem, z_rsem,
    lrs_ssem, lrs_rsem, lag_ssem, lag_rsem, a_ssem, a_rsem, b_ssem, b_rsem,
    out_sem, out_ssem, out_rsem,
):
    R, L, C, Q, T, A, B, H, HQ, HL, W = dims
    RC = R // C
    LQ = L // Q
    SB = B // W
    LP = T * (T - 1) // 2
    AP = A * (A - 1) // 2
    row = lax.axis_index("row")
    layer = lax.axis_index("layer")
    col = lax.axis_index("col")

    def ahead(axis_index, step, size):
        return lax.rem(axis_index + step, size)

    def behind(axis_index, step, size):
        return lax.rem(axis_index + size - step, size)

    loads = []

    def load(src, dst):
        copy = pltpu.make_async_copy(src, dst, load_sem.at[len(loads)])
        copy.start()
        loads.append(copy)
        return copy

    my_cols = pl.ds(pl.multiple_of(col * H, H), H)
    ld_rhs = [load(leaf_rhs.at[0, 0, :, my_cols], rhs_in.at[0])]
    ld_inv = load(leaf_inv.at[0, :, pl.ds(row * SB, SB)], inv)
    ld_leaf = [
        load(leaf_tiles.at[0, :, :, pl.ds(j * B, B)], leaf_m.at[:, col * RC + j])
        for j in range(RC)
    ]
    for t in range(1, T):
        ld_rhs.append(load(leaf_rhs.at[0, t, :, my_cols], rhs_in.at[t]))
    ld_cross = [
        load(cross_tiles.at[0, :, :, :, pl.ds(j * B, B)], cross_m.at[:, :, col * RC + j])
        for j in range(RC)
    ]
    ld_top = [
        load(top_tiles.at[:, :, pl.ds(j * B, B)], top_m.at[:, col * RC + j])
        for j in range(RC)
    ]
    ld_arhs = load(anc_rhs.at[:, :, my_cols], arhs_in)
    ld_ainv = load(anc_inv.at[:, pl.ds(row * SB, SB)], ainv)

    barrier = pltpu.get_barrier_semaphore()
    for name, mine, size in (("row", row, R), ("layer", layer, L), ("col", col, C)):
        for step in range(1, size):
            pl.semaphore_signal(
                barrier, inc=1, device_id={name: ahead(mine, step, size)}, device_id_type=MESH
            )

    def remote(src, dst, ssem, rsem, name, target):
        return pltpu.make_async_remote_copy(
            src_ref=src, dst_ref=dst, send_sem=ssem, recv_sem=rsem,
            device_id={name: target}, device_id_type=MESH,
        )

    def y_copy(t, q, k, source):
        block = ybuf.at[t, q, source]
        return remote(block, block, y_ssem.at[t, q, k], y_rsem.at[t, q, k], "row", ahead(row, k, R))

    def z_copy(a, k, source):
        block = zbuf.at[a, source]
        return remote(block, block, z_ssem.at[a, k], z_rsem.at[a, k], "row", ahead(row, k, R))

    def a_copy(a, k):
        return remote(
            asend.at[a, k], arecv.at[a, k], a_ssem.at[a, k], a_rsem.at[a, k], "row", ahead(row, k, R)
        )

    def b_copy(t, q, k):
        return remote(
            bsend.at[t, q, k], brecv.at[t, q, k], b_ssem.at[t, q, k], b_rsem.at[t, q, k],
            "row", ahead(row, k, R),
        )

    def lrs_copy(k):
        target = ahead(layer, k, L)
        return remote(zs.at[target], zr.at[k], lrs_ssem.at[k], lrs_rsem.at[k], "layer", target)

    def lag_copy(a, k, source):
        block = xanc.at[a, source]
        return remote(
            block, block, lag_ssem.at[a, k], lag_rsem.at[a, k], "layer", ahead(layer, k, L)
        )

    def tile_copy(slot, k, source):
        held = pl.ds(source * RC, RC)
        if slot < LP:
            block = leaf_m.at[slot, held]
        elif slot < LP + A * T:
            block = cross_m.at[(slot - LP) // T, (slot - LP) % T, held]
        else:
            block = top_m.at[slot - LP - A * T, held]
        return remote(
            block, block, col_ssem.at[slot, k], col_rsem.at[slot, k], "col", ahead(col, k, C)
        )

    def tiles_arrive(slot):
        for k in range(1, C):
            tile_copy(slot, k, behind(col, k, C)).wait_recv()

    def send_tiles(slot):
        for k in range(1, C):
            tile_copy(slot, k, col).start()

    def each(start, stop, action):
        def body(index, carry):
            action(index)
            return carry

        loop(start, stop, body, 0)

    def mask(ref, lead, pattern, lead_pattern):
        def one(j):
            for i in range(SB):
                for n in range(SB):
                    bit = pattern[(*lead_pattern, i, j * SB + n)].astype(F32)
                    spread = jnp.full((W, W), bit, F32).astype(BF16)
                    at = (*lead, col * RC + j, pl.ds(i * W, W), pl.ds(n * W, W))
                    ref[at] = ref[at] * spread

        each(0, RC, one)

    def send_y(t, q):
        each(1, R, lambda k: y_copy(t, q, k, row).start())

    def turn_rhs(t):
        ld_rhs[t].wait()
        rhs_t[t] = rhs_in[t].T.reshape(Q, HQ, B)

    turn_rhs(0)
    ld_inv.wait()
    for q in range(Q):
        ybuf[0, q, row] = solve(inv, 0, rhs_t[0, q], False).astype(BF16)
    pl.semaphore_wait(barrier, (R - 1) + (L - 1) + (C - 1))
    for q in range(Q):
        send_y(0, q)
    for copy in ld_leaf:
        copy.wait()
    for slot in range(LP):
        mask(leaf_m, (slot,), leaf_pat, (0, slot))
        send_tiles(slot)
    for t in range(1, T):
        turn_rhs(t)
    for copy in ld_cross:
        copy.wait()
    for a in range(A):
        for t in range(T):
            mask(cross_m, (a, t), cross_pat, (0, a, t))
            send_tiles(LP + a * T + t)
    for copy in ld_top:
        copy.wait()
    for slot in range(AP):
        mask(top_m, (slot,), top_pat, (slot,))
        send_tiles(LP + A * T + slot)
    ld_arhs.wait()
    ld_ainv.wait()
    for a in range(A):
        arhs_t[a] = arhs_in[a].T.reshape(L, HL, B)

    def product(vectors, tiles, form=NT):
        return loop(
            1, R,
            lambda k, total: total + dot(vectors(k), tiles(k), form),
            dot(vectors(0), tiles(0), form),
        )

    arrived = set()

    def need(slot):
        if slot not in arrived:
            arrived.add(slot)
            tiles_arrive(slot)

    zero = jnp.zeros((HQ, B), F32)

    def fold_forward(s, q):
        for t in range(s + 2, T):
            need(pair_index(t, s))
            term = product(lambda k: ybuf[s, q, k], lambda k: leaf_m[pair_index(t, s), k])
            fsum[t, q] = term if s == 0 else fsum[t, q] + term
        for a in range(A):
            need(LP + a * T + s)
            term = product(lambda k: ybuf[s, q, k], lambda k: cross_m[a, s, k])
            here = pl.ds(q * LQ, LQ)
            if s > 0:
                term = term + csum[a, here].reshape(HQ, B)
            csum[a, here] = term.reshape(LQ, HL, B)

    for t in range(1, T):
        for q in range(Q):
            need(pair_index(t, t - 1))

            def arriving(k, total):
                source = behind(row, k, R)
                y_copy(t - 1, q, k, source).wait_recv()
                return total + dot(ybuf[t - 1, q, source], leaf_m[pair_index(t, t - 1), source], NT)

            residual = rhs_t[t, q]
            if t > 1:
                residual = residual - fsum[t, q]
            own = dot(ybuf[t - 1, q, row], leaf_m[pair_index(t, t - 1), row], NT)
            residual = residual - loop(1, R, arriving, own)
            ybuf[t, q, row] = solve(inv, t, residual, False).astype(BF16)
            send_y(t, q)
        for q in range(Q):
            fold_forward(t - 1, q)

    last = T - 1
    for q in range(Q):
        each(1, R, lambda k: y_copy(last, q, k, behind(row, k, R)).wait_recv())
        fold_forward(last, q)
        for a in range(A):
            here = pl.ds(q * LQ, LQ)
            zs[here, a] = csum[a, here].astype(BF16)

    each(1, L, lambda k: lrs_copy(k).start())

    def add_layer(k, totals):
        lrs_copy(k).wait_recv()
        return tuple(totals[a] + zr[k, a].astype(F32) for a in range(A))

    for slot in range(AP):
        need(LP + A * T + slot)
    sums = loop(1, L, add_layer, tuple(csum[a, layer] for a in range(A)))
    for a in range(A):
        residual = arhs_t[a, layer] - sums[a]
        for s in range(a):
            if s == a - 1:
                each(1, R, lambda k: z_copy(s, k, behind(row, k, R)).wait_recv())
            residual = residual - product(
                lambda k: zbuf[s, k], lambda k: top_m[pair_index(a, s), k]
            )
        zbuf[a, row] = solve(ainv, a, residual, False).astype(BF16)
        if a < A - 1:
            each(1, R, lambda k: z_copy(a, k, row).start())
    for a in range(A - 1, -1, -1):
        residual = zbuf[a, row].astype(F32)
        if a < A - 1:

            def partial(target):
                total = None
                for b in range(a + 1, A):
                    term = dot(xanc[b, layer], top_m[pair_index(b, a), target], NN)
                    total = term if total is None else total + term
                return total

            def send_part(k):
                asend[a, k] = partial(ahead(row, k, R)).astype(BF16)
                a_copy(a, k).start()

            each(1, R, send_part)

            def add_part(k, total):
                a_copy(a, k).wait_recv()
                return total + arecv[a, k].astype(F32)

            residual = residual - loop(1, R, add_part, partial(row))
        xanc[a, layer] = solve(ainv, a, residual, True).astype(BF16)
        each(1, L, lambda k: lag_copy(a, k, layer).start())

    def out_copies(slot, k):
        if slot < T:
            held = leaf_out.at[0, slot, :, my_cols]
        else:
            held = anc_out.at[slot - T, :, my_cols]
        return remote(
            stage.at[slot], held, out_ssem.at[slot, k], out_rsem.at[slot, k], "col", ahead(col, k, C)
        )

    def out_arrival(slot, k):
        theirs = pl.ds(pl.multiple_of(behind(col, k, C) * H, H), H)
        if slot < T:
            held = leaf_out.at[0, slot, :, theirs]
        else:
            held = anc_out.at[slot - T, :, theirs]
        return remote(
            stage.at[slot], held, out_ssem.at[slot, k], out_rsem.at[slot, k], "col", ahead(col, k, C)
        )

    def out_local(slot):
        held = leaf_out.at[0, slot, :, my_cols] if slot < T else anc_out.at[slot - T, :, my_cols]
        return pltpu.make_async_copy(stage.at[slot], held, out_sem.at[slot])

    def emit(slot, value):
        stage[slot] = value.astype(F32).T.astype(BF16)
        for k in range(1, C):
            out_copies(slot, k).start()
        out_local(slot).start()

    def anc_chunk(a, q):
        return xanc[a, pl.ds(q * LQ, LQ)].reshape(HQ, B)

    def fold_cross(a, t, first):
        for q in range(Q):

            def one(k):
                term = dot(anc_chunk(a, q), cross_m[a, t, k], NN)
                bsum[t, q, k] = term if first else bsum[t, q, k] + term

            each(0, R, one)

    def start_level(t, q):
        def value(target):
            total = bsum[t, q, target]
            if t == T - 1:
                return total + dot(anc_chunk(0, q), cross_m[0, t, target], NN)
            return total + dot(xbuf[t + 1, q], leaf_m[pair_index(t + 1, t), target], NN)

        def send_part(k):
            bsend[t, q, k] = value(ahead(row, k, R)).astype(BF16)
            b_copy(t, q, k).start()

        each(1, R, send_part)
        bown[t, q] = value(row)

    for a in range(A - 1, 0, -1):
        each(1, L, lambda k: lag_copy(a, k, behind(layer, k, L)).wait_recv())
        for t in range(T - 1, -1, -1):
            fold_cross(a, t, a == A - 1)
    each(1, L, lambda k: lag_copy(0, k, behind(layer, k, L)).wait_recv())
    for q in range(Q):
        start_level(T - 1, q)
    for t in range(T - 2, -1, -1):
        fold_cross(0, t, A == 1)
    for a in range(A):
        emit(T + a, xanc[a].reshape(H, B))
    for t in range(T - 1, -1, -1):
        for q in range(Q):

            def add_part(k, total):
                b_copy(t, q, k).wait_recv()
                return total + brecv[t, q, k].astype(F32)

            residual = ybuf[t, q, row].astype(F32) - loop(1, R, add_part, bown[t, q])
            xbuf[t, q] = solve(inv, t, residual, True).astype(BF16)
            if t > 0:
                start_level(t - 1, q)
        emit(t, xbuf[t].reshape(H, B))
        for lower in range(t - 1):
            for q in range(Q):

                def one(k):
                    bsum[lower, q, k] += dot(xbuf[t, q], leaf_m[pair_index(t, lower), k], NN)

                each(0, R, one)

    for slot in range(LP + A * T + AP):
        for k in range(1, C):
            tile_copy(slot, k, col).wait_send()
    for t in range(T):
        for q in range(Q):
            each(1, R, lambda k: y_copy(t, q, k, row).wait_send())
            each(1, R, lambda k: b_copy(t, q, k).wait_send())
    for a in range(A - 1):
        each(1, R, lambda k: z_copy(a, k, row).wait_send())
        each(1, R, lambda k: a_copy(a, k).wait_send())
    each(1, L, lambda k: lrs_copy(k).wait_send())
    for a in range(A):
        each(1, L, lambda k: lag_copy(a, k, layer).wait_send())
    for slot in range(T + A):
        out_local(slot).wait()
        for k in range(1, C):
            out_copies(slot, k).wait_send()
            out_arrival(slot, k).wait_recv()


def local(R, L, C, *arrays):
    leaf_rhs, anc_rhs = arrays[:2]
    T = leaf_rhs.shape[1]
    A = anc_rhs.shape[0]
    B = leaf_rhs.shape[2]
    H = leaf_rhs.shape[3] // C
    W = arrays[8].shape[-1]
    Q = 2 if R <= 4 and L % 2 == 0 else 1
    HQ, HL = H // Q, H // L
    SB = B // W
    LP, AP = T * (T - 1) // 2, A * (A - 1) // 2
    dims = (R, L, C, Q, T, A, B, H, HQ, HL, W)
    vmem = pltpu.VMEM
    dma = pltpu.SemaphoreType.DMA
    slots = LP + A * T + AP
    scratch = [
        vmem((T, B, H), F32), vmem((A, B, H), F32),
        vmem((T, SB, W, W), BF16), vmem((A, SB, W, W), BF16),
        vmem((T, Q, HQ, B), F32), vmem((A, L, HL, B), F32),
        vmem((LP, R, B, B), BF16), vmem((A, T, R, B, B), BF16), vmem((AP, R, B, B), BF16),
        vmem((T, Q, R, HQ, B), BF16), vmem((T, Q, HQ, B), F32), vmem((A, L, HL, B), F32),
        vmem((L, A, HL, B), BF16), vmem((L, A, HL, B), BF16),
        vmem((A, R, HL, B), BF16), vmem((A, L, HL, B), BF16),
        vmem((A, R, HL, B), BF16), vmem((A, R, HL, B), BF16),
        vmem((T, Q, R, HQ, B), F32), vmem((T, Q, HQ, B), F32),
        vmem((T, Q, R, HQ, B), BF16), vmem((T, Q, R, HQ, B), BF16),
        vmem((T, Q, HQ, B), BF16), vmem((T + A, B, H), BF16),
        dma((T + 3 + 3 * (R // C),)),
        dma((slots, C)), dma((slots, C)),
        dma((T, Q, R)), dma((T, Q, R)), dma((A, R)), dma((A, R)),
        dma((L,)), dma((L,)), dma((A, L)), dma((A, L)),
        dma((A, R)), dma((A, R)), dma((T, Q, R)), dma((T, Q, R)),
        dma((T + A,)), dma((T + A, C)), dma((T + A, C)),
    ]
    anywhere = pl.BlockSpec(memory_space=pl.ANY)
    scalars = pl.BlockSpec(memory_space=pltpu.SMEM)
    return pl.pallas_call(
        functools.partial(kernel, dims),
        out_shape=(
            jax.ShapeDtypeStruct(leaf_rhs.shape, BF16),
            jax.ShapeDtypeStruct(anc_rhs.shape, BF16),
        ),
        in_specs=[anywhere] * 5 + [scalars] * 3 + [anywhere] * 2,
        out_specs=(anywhere, anywhere),
        scratch_shapes=scratch,
        compiler_params=pltpu.CompilerParams(
            collective_id=0, has_side_effects=True, vmem_limit_bytes=56 * 1024 * 1024
        ),
    )(*arrays)


def solution(mesh):
    in_specs = (
        P("layer", None, "row", None),
        P(None, "row", None),
        P("layer", None, "row", "col"),
        P("layer", None, None, "row", "col"),
        P(None, "row", "col"),
        P("layer", None, "row", "col"),
        P("layer", None, None, "row", "col"),
        P(None, "row", "col"),
        P("layer", None, None, None, None),
        P(),
    )
    out_specs = (P("layer", None, "row", None), P(None, "row", None))
    sizes = mesh.shape
    return jax.shard_map(
        functools.partial(local, sizes["row"], sizes["layer"], sizes["col"]),
        mesh=mesh, in_specs=in_specs, out_specs=out_specs, check_vma=False,
    )
```

time: 375 us -> 56.6 us (0.15)
  waiting for transfers between devices: 237 us -> 0 us
  blocking collectives: 57.2 us -> 0 us
  Pallas kernels: 0 us -> 52.3 us
  matrix products: 33.1 us -> 0 us
  local copies, waits for them, and re-layouts: 18.2 us -> 3.44 us
  between operations: 14.5 us -> 0.64 us
  other arithmetic: 13.4 us -> 0 us
    psum x6 -> x0, waiting for transfers between devices: 233 us -> none  [the longest x4 164 us: finish(): lax.psum(partial_value.astype(jnp.bfloat16), 'row').astype(jnp.float32)]
    all_gather x11 -> x0, blocking collectives: 57.2 us -> none  [the longest x3 32 us: local(): whole = lax.all_gather(row_block, 'row', axis=0, tiled=True)]
    pallas_call x0 -> x1, Pallas kernels: none -> 52.3 us  [local(): pl.pallas_call(functools.partial(kernel, dims), out_shape=(jax.ShapeDtype...]
    dot_general x29 -> x0, matrix products: 33.1 us -> none  [the longest x10 12.8 us: backward_product(): lax.dot_general(masked, vector, (((0,), (0,)), ((), ())), preferred_eleme...]
    convert_element_type x10 -> x0, other arithmetic: 8.13 us -> none  [the longest x6 7.07 us: solve_blocks(): residual.astype(jnp.bfloat16).reshape(number, tile_width, residual.shape[1])]
    slice x4 -> x0, local copies, waits for them, and re-layouts: 6.59 us -> none  [the longest x2 2.74 us: local(): rhs_rows = leaf_rhs[0, target]]
    reduce_scatter x2 -> x0, waiting for transfers between devices: 4.12 us -> none  [local(): lax.psum_scatter(partial_value.astype(jnp.bfloat16), 'col', scatter_dimen...]
  transfers between devices with their start and end apart: 8 -> 0, of which waited for: 7 -> 0; matrix products, arithmetic and copies ran while one was open for 7% -> 0% of each run, Pallas kernels for 0% -> 0%
where the time goes in v1:
time: 56.6 us; the launch traced here: 56.4 us
  Pallas kernels  52.3 us (92%)
  local copies, waits for them, and re-layouts  3.44 us (6%)
  between operations  0.64 us (1%)
    pallas_call x1, Pallas kernels, local(): pl.pallas_call(functools.partial(kernel, dims), out_shape=(jax.ShapeDtype...  52.3 us
    unnamed x2, local copies, waits for them, and re-layouts  3.44 us

profile of v1, /device:TPU:0, one launch (start us, length us, event | category | flops | bytes accessed | tf_op | source)
XLA Modules:
  0.0 56.4 jit_solution(11029829676553304501)
XLA Ops:
  0.6 52.3 %shard_map.113 = (bf16[1,3,256,256]{3,2,1,0:T(8,128)(2,1)}, bf16[2,256,256]{2,1,0:T(8,128)(2,1)}) custom-call(f32[1,3,256,256]{3,2,1,0:T(8,128)} %leaf_rhs.1, f32[2,256,256]{2,1,0:T(8,128)} %anc_rhs.1, bf16[1,3,256,512]{3,2,1,0:T(8,128)(2,1)} %leaf_tiles.1, bf16[1,2,3,256,512]{4,3,2,1,0:T(8,128)(2,1)} %cross_tiles.1, bf16[1,256,512]{2,1,0:T(8,128)(2,1)} %top_tiles.1, ...), custom_call_target="tpu_custom_call" | custom-call | tf_op jit(solution)/shard_map/pallas_call | solution.py:460
  53.0 1.8 %copy.14 = bf16[1,3,256,256]{3,2,1,0:T(8,128)(2,1)} copy(bf16[1,3,256,256]{3,2,1,0:T(8,128)(2,1)} %get-tuple-element.4) | data formatting | bytes 786432
  54.7 1.7 %copy.15 = bf16[2,256,256]{2,1,0:T(8,128)(2,1)} copy(bf16[2,256,256]{2,1,0:T(8,128)(2,1)} %get-tuple-element.5) | data formatting | bytes 524288

commit v2 on v1

--- a/solution.py
+++ b/solution.py
@@ -48,10 +48,10 @@
     leaf_out, anc_out,
     rhs_in, arhs_in, inv, ainv, rhs_t, arhs_t, leaf_m, cross_m, top_m,
     ybuf, fsum, csum, zs, zr, zbuf, xanc, asend, arecv,
-    bsum, bown, bsend, brecv, xbuf, stage,
+    bsum, bown, bsend, brecv, xbuf,
     load_sem, col_ssem, col_rsem, y_ssem, y_rsem, z_ssem, z_rsem,
     lrs_ssem, lrs_rsem, lag_ssem, lag_rsem, a_ssem, a_rsem, b_ssem, b_rsem,
-    out_sem, out_ssem, out_rsem,
+    out_ssem, out_rsem,
 ):
     R, L, C, Q, T, A, B, H, HQ, HL, W = dims
     RC = R // C
@@ -68,6 +68,20 @@
 
     def behind(axis_index, step, size):
         return lax.rem(axis_index + size - step, size)
+
+    binary = R & (R - 1) == 0
+
+    def row_to(step):
+        if not binary:
+            return ahead(row, step, R)
+        total, place = 0, 1
+        while place < R:
+            total = total + lax.rem(lax.div(row, place) + step // place, 2) * place
+            place *= 2
+        return total
+
+    def row_from(step):
+        return row_to(step) if binary else behind(row, step, R)
 
     loads = []
 
@@ -112,26 +126,28 @@
 
     def y_copy(t, q, k, source):
         block = ybuf.at[t, q, source]
-        return remote(block, block, y_ssem.at[t, q, k], y_rsem.at[t, q, k], "row", ahead(row, k, R))
+        return remote(block, block, y_ssem.at[t, q, k], y_rsem.at[t, q, k], "row", row_to(k))
 
     def z_copy(a, k, source):
         block = zbuf.at[a, source]
-        return remote(block, block, z_ssem.at[a, k], z_rsem.at[a, k], "row", ahead(row, k, R))
+        return remote(block, block, z_ssem.at[a, k], z_rsem.at[a, k], "row", row_to(k))
 
     def a_copy(a, k):
         return remote(
-            asend.at[a, k], arecv.at[a, k], a_ssem.at[a, k], a_rsem.at[a, k], "row", ahead(row, k, R)
+            asend.at[a, k], arecv.at[a, k], a_ssem.at[a, k], a_rsem.at[a, k], "row", row_to(k)
         )
 
     def b_copy(t, q, k):
         return remote(
             bsend.at[t, q, k], brecv.at[t, q, k], b_ssem.at[t, q, k], b_rsem.at[t, q, k],
-            "row", ahead(row, k, R),
-        )
-
-    def lrs_copy(k):
+            "row", row_to(k),
+        )
+
+    def lrs_copy(a, k):
         target = ahead(layer, k, L)
-        return remote(zs.at[target], zr.at[k], lrs_ssem.at[k], lrs_rsem.at[k], "layer", target)
+        return remote(
+            zs.at[a, target], zr.at[a, k], lrs_ssem.at[a, k], lrs_rsem.at[a, k], "layer", target
+        )
 
     def lag_copy(a, k, source):
         block = xanc.at[a, source]
@@ -178,7 +194,7 @@
         each(0, RC, one)
 
     def send_y(t, q):
-        each(1, R, lambda k: y_copy(t, q, k, row).start())
+        each(1, R, lambda k: y_copy(t, q, R - k, row).start())
 
     def turn_rhs(t):
         ld_rhs[t].wait()
@@ -228,27 +244,28 @@
             arrived.add(slot)
             tiles_arrive(slot)
 
-    zero = jnp.zeros((HQ, B), F32)
-
-    def fold_forward(s, q):
+    def whole(ref, lead, k):
+        return ref[(lead, slice(None), k)].reshape(H, B)
+
+    def fold_leaf(s):
         for t in range(s + 2, T):
             need(pair_index(t, s))
-            term = product(lambda k: ybuf[s, q, k], lambda k: leaf_m[pair_index(t, s), k])
-            fsum[t, q] = term if s == 0 else fsum[t, q] + term
-        for a in range(A):
-            need(LP + a * T + s)
-            term = product(lambda k: ybuf[s, q, k], lambda k: cross_m[a, s, k])
-            here = pl.ds(q * LQ, LQ)
-            if s > 0:
-                term = term + csum[a, here].reshape(HQ, B)
-            csum[a, here] = term.reshape(LQ, HL, B)
+            term = product(lambda k: whole(ybuf, s, k), lambda k: leaf_m[pair_index(t, s), k])
+            term = term.reshape(Q, HQ, B)
+            fsum[t] = term if s == 0 else fsum[t] + term
+
+    def fold_ancestor(s, a):
+        need(LP + a * T + s)
+        term = product(lambda k: whole(ybuf, s, k), lambda k: cross_m[a, s, k])
+        term = term.reshape(L, HL, B)
+        csum[a] = term if s == 0 else csum[a] + term
 
     for t in range(1, T):
         for q in range(Q):
             need(pair_index(t, t - 1))
 
             def arriving(k, total):
-                source = behind(row, k, R)
+                source = row_from(k)
                 y_copy(t - 1, q, k, source).wait_recv()
                 return total + dot(ybuf[t - 1, q, source], leaf_m[pair_index(t, t - 1), source], NT)
 
@@ -259,37 +276,38 @@
             residual = residual - loop(1, R, arriving, own)
             ybuf[t, q, row] = solve(inv, t, residual, False).astype(BF16)
             send_y(t, q)
-        for q in range(Q):
-            fold_forward(t - 1, q)
+        fold_leaf(t - 1)
+        for a in range(A):
+            fold_ancestor(t - 1, a)
 
     last = T - 1
     for q in range(Q):
-        each(1, R, lambda k: y_copy(last, q, k, behind(row, k, R)).wait_recv())
-        fold_forward(last, q)
-        for a in range(A):
-            here = pl.ds(q * LQ, LQ)
-            zs[here, a] = csum[a, here].astype(BF16)
-
-    each(1, L, lambda k: lrs_copy(k).start())
-
-    def add_layer(k, totals):
-        lrs_copy(k).wait_recv()
-        return tuple(totals[a] + zr[k, a].astype(F32) for a in range(A))
+        each(1, R, lambda k: y_copy(last, q, k, row_from(k)).wait_recv())
+    for a in range(A):
+        fold_ancestor(last, a)
+        zs[a] = csum[a].astype(BF16)
+        each(1, L, lambda k: lrs_copy(a, k).start())
+
+    def layer_sum(a):
+        def add_layer(k, total):
+            lrs_copy(a, k).wait_recv()
+            return total + zr[a, k].astype(F32)
+
+        return loop(1, L, add_layer, csum[a, layer])
 
     for slot in range(AP):
         need(LP + A * T + slot)
-    sums = loop(1, L, add_layer, tuple(csum[a, layer] for a in range(A)))
-    for a in range(A):
-        residual = arhs_t[a, layer] - sums[a]
+    for a in range(A):
+        residual = arhs_t[a, layer] - layer_sum(a)
         for s in range(a):
             if s == a - 1:
-                each(1, R, lambda k: z_copy(s, k, behind(row, k, R)).wait_recv())
+                each(1, R, lambda k: z_copy(s, k, row_from(k)).wait_recv())
             residual = residual - product(
                 lambda k: zbuf[s, k], lambda k: top_m[pair_index(a, s), k]
             )
         zbuf[a, row] = solve(ainv, a, residual, False).astype(BF16)
         if a < A - 1:
-            each(1, R, lambda k: z_copy(a, k, row).start())
+            each(1, R, lambda k: z_copy(a, R - k, row).start())
     for a in range(A - 1, -1, -1):
         residual = zbuf[a, row].astype(F32)
         if a < A - 1:
@@ -302,10 +320,10 @@
                 return total
 
             def send_part(k):
-                asend[a, k] = partial(ahead(row, k, R)).astype(BF16)
+                asend[a, k] = partial(row_to(k)).astype(BF16)
                 a_copy(a, k).start()
 
-            each(1, R, send_part)
+            each(1, R, lambda k: send_part(R - k))
 
             def add_part(k, total):
                 a_copy(a, k).wait_recv()
@@ -315,46 +333,37 @@
         xanc[a, layer] = solve(ainv, a, residual, True).astype(BF16)
         each(1, L, lambda k: lag_copy(a, k, layer).start())
 
-    def out_copies(slot, k):
+    def out_place(slot, owner):
+        cols = pl.ds(pl.multiple_of(owner * H, H), H)
+        return leaf_out.at[0, slot, :, cols] if slot < T else anc_out.at[slot - T, :, cols]
+
+    def out_copy(slot, k, source):
+        block = out_place(slot, source)
+        return remote(
+            block, block, out_ssem.at[slot, k], out_rsem.at[slot, k], "col", ahead(col, k, C)
+        )
+
+    def emit(slot, value):
+        turned = value.astype(F32).T.astype(BF16)
         if slot < T:
-            held = leaf_out.at[0, slot, :, my_cols]
+            leaf_out[0, slot, :, my_cols] = turned
         else:
-            held = anc_out.at[slot - T, :, my_cols]
-        return remote(
-            stage.at[slot], held, out_ssem.at[slot, k], out_rsem.at[slot, k], "col", ahead(col, k, C)
-        )
-
-    def out_arrival(slot, k):
-        theirs = pl.ds(pl.multiple_of(behind(col, k, C) * H, H), H)
-        if slot < T:
-            held = leaf_out.at[0, slot, :, theirs]
-        else:
-            held = anc_out.at[slot - T, :, theirs]
-        return remote(
-            stage.at[slot], held, out_ssem.at[slot, k], out_rsem.at[slot, k], "col", ahead(col, k, C)
-        )
-
-    def out_local(slot):
-        held = leaf_out.at[0, slot, :, my_cols] if slot < T else anc_out.at[slot - T, :, my_cols]
-        return pltpu.make_async_copy(stage.at[slot], held, out_sem.at[slot])
-
-    def emit(slot, value):
-        stage[slot] = value.astype(F32).T.astype(BF16)
+            anc_out[slot - T, :, my_cols] = turned
         for k in range(1, C):
-            out_copies(slot, k).start()
-        out_local(slot).start()
+            out_copy(slot, k, col).start()
 
     def anc_chunk(a, q):
         return xanc[a, pl.ds(q * LQ, LQ)].reshape(HQ, B)
 
-    def fold_cross(a, t, first):
-        for q in range(Q):
-
-            def one(k):
-                term = dot(anc_chunk(a, q), cross_m[a, t, k], NN)
-                bsum[t, q, k] = term if first else bsum[t, q, k] + term
-
-            each(0, R, one)
+    def fold_back(t, vector, tiles, first=False):
+        def one(k):
+            term = dot(vector, tiles(k), NN).reshape(Q, HQ, B)
+            bsum[t, :, k] = term if first else bsum[t, :, k] + term
+
+        each(0, R, one)
+
+    def fold_cross(a, t):
+        fold_back(t, xanc[a].reshape(H, B), lambda k: cross_m[a, t, k], a == A - 1)
 
     def start_level(t, q):
         def value(target):
@@ -364,21 +373,21 @@
             return total + dot(xbuf[t + 1, q], leaf_m[pair_index(t + 1, t), target], NN)
 
         def send_part(k):
-            bsend[t, q, k] = value(ahead(row, k, R)).astype(BF16)
+            bsend[t, q, k] = value(row_to(k)).astype(BF16)
             b_copy(t, q, k).start()
 
-        each(1, R, send_part)
+        each(1, R, lambda k: send_part(R - k))
         bown[t, q] = value(row)
 
     for a in range(A - 1, 0, -1):
         each(1, L, lambda k: lag_copy(a, k, behind(layer, k, L)).wait_recv())
-        for t in range(T - 1, -1, -1):
-            fold_cross(a, t, a == A - 1)
+        fold_cross(a, T - 1)
     each(1, L, lambda k: lag_copy(0, k, behind(layer, k, L)).wait_recv())
     for q in range(Q):
         start_level(T - 1, q)
     for t in range(T - 2, -1, -1):
-        fold_cross(0, t, A == 1)
+        for a in range(A - 1, -1, -1):
+            fold_cross(a, t)
     for a in range(A):
         emit(T + a, xanc[a].reshape(H, B))
     for t in range(T - 1, -1, -1):
@@ -394,12 +403,7 @@
                 start_level(t - 1, q)
         emit(t, xbuf[t].reshape(H, B))
         for lower in range(t - 1):
-            for q in range(Q):
-
-                def one(k):
-                    bsum[lower, q, k] += dot(xbuf[t, q], leaf_m[pair_index(t, lower), k], NN)
-
-                each(0, R, one)
+            fold_back(lower, xbuf[t].reshape(H, B), lambda k: leaf_m[pair_index(t, lower), k])
 
     for slot in range(LP + A * T + AP):
         for k in range(1, C):
@@ -411,14 +415,13 @@
     for a in range(A - 1):
         each(1, R, lambda k: z_copy(a, k, row).wait_send())
         each(1, R, lambda k: a_copy(a, k).wait_send())
-    each(1, L, lambda k: lrs_copy(k).wait_send())
-    for a in range(A):
+    for a in range(A):
+        each(1, L, lambda k: lrs_copy(a, k).wait_send())
         each(1, L, lambda k: lag_copy(a, k, layer).wait_send())
     for slot in range(T + A):
-        out_local(slot).wait()
         for k in range(1, C):
-            out_copies(slot, k).wait_send()
-            out_arrival(slot, k).wait_recv()
+            out_copy(slot, k, col).wait_send()
+            out_copy(slot, k, behind(col, k, C)).wait_recv()
 
 
 def local(R, L, C, *arrays):
@@ -442,29 +445,29 @@
         vmem((T, Q, HQ, B), F32), vmem((A, L, HL, B), F32),
         vmem((LP, R, B, B), BF16), vmem((A, T, R, B, B), BF16), vmem((AP, R, B, B), BF16),
         vmem((T, Q, R, HQ, B), BF16), vmem((T, Q, HQ, B), F32), vmem((A, L, HL, B), F32),
-        vmem((L, A, HL, B), BF16), vmem((L, A, HL, B), BF16),
+        vmem((A, L, HL, B), BF16), vmem((A, L, HL, B), BF16),
         vmem((A, R, HL, B), BF16), vmem((A, L, HL, B), BF16),
         vmem((A, R, HL, B), BF16), vmem((A, R, HL, B), BF16),
         vmem((T, Q, R, HQ, B), F32), vmem((T, Q, HQ, B), F32),
         vmem((T, Q, R, HQ, B), BF16), vmem((T, Q, R, HQ, B), BF16),
-        vmem((T, Q, HQ, B), BF16), vmem((T + A, B, H), BF16),
+        vmem((T, Q, HQ, B), BF16),
         dma((T + 3 + 3 * (R // C),)),
         dma((slots, C)), dma((slots, C)),
         dma((T, Q, R)), dma((T, Q, R)), dma((A, R)), dma((A, R)),
-        dma((L,)), dma((L,)), dma((A, L)), dma((A, L)),
+        dma((A, L)), dma((A, L)), dma((A, L)), dma((A, L)),
         dma((A, R)), dma((A, R)), dma((T, Q, R)), dma((T, Q, R)),
-        dma((T + A,)), dma((T + A, C)), dma((T + A, C)),
+        dma((T + A, C)), dma((T + A, C)),
     ]
     anywhere = pl.BlockSpec(memory_space=pl.ANY)
     scalars = pl.BlockSpec(memory_space=pltpu.SMEM)
     return pl.pallas_call(
         functools.partial(kernel, dims),
         out_shape=(
-            jax.ShapeDtypeStruct(leaf_rhs.shape, BF16),
-            jax.ShapeDtypeStruct(anc_rhs.shape, BF16),
+            vmem(leaf_rhs.shape, BF16),
+            vmem(anc_rhs.shape, BF16),
         ),
         in_specs=[anywhere] * 5 + [scalars] * 3 + [anywhere] * 2,
-        out_specs=(anywhere, anywhere),
+        out_specs=(pl.BlockSpec(memory_space=vmem),) * 2,
         scratch_shapes=scratch,
         compiler_params=pltpu.CompilerParams(
             collective_id=0, has_side_effects=True, vmem_limit_bytes=56 * 1024 * 1024

time: 56.6 us -> 52.7 us (0.931)
  local copies, waits for them, and re-layouts: 3.44 us -> 1.45 us
  Pallas kernels: 52.3 us -> 50.4 us
    unnamed x2, local copies, waits for them, and re-layouts: 3.44 us -> 1.45 us
    pallas_call x1, Pallas kernels: 52.3 us -> 50.4 us  [local(): pl.pallas_call(functools.partial(kernel, dims), out_shape=(vmem(leaf_rhs....]
where the time goes in v2:
time: 52.7 us; the launch traced here: 52.5 us
  Pallas kernels  50.4 us (96%)
  local copies, waits for them, and re-layouts  1.45 us (3%)
  between operations  0.64 us (1%)
    pallas_call x1, Pallas kernels, local(): pl.pallas_call(functools.partial(kernel, dims), out_shape=(vmem(leaf_rhs....  50.4 us
    unnamed x2, local copies, waits for them, and re-layouts  1.45 us

profile of v2, /device:TPU:0, one launch (start us, length us, event | category | flops | bytes accessed | tf_op | source)
XLA Modules:
  0.0 52.5 jit_solution(15975540820555429721)
XLA Ops:
  0.6 50.4 %shard_map.113 = (bf16[1,3,256,256]{3,2,1,0:T(8,128)(2,1)S(1)}, bf16[2,256,256]{2,1,0:T(8,128)(2,1)S(1)}) custom-call(f32[1,3,256,256]{3,2,1,0:T(8,128)} %leaf_rhs.1, f32[2,256,256]{2,1,0:T(8,128)} %anc_rhs.1, bf16[1,3,256,512]{3,2,1,0:T(8,128)(2,1)} %leaf_tiles.1, bf16[1,2,3,256,512]{4,3,2,1,0:T(8,128)(2,1)} %cross_tiles.1, bf16[1,256,512]{2,1,0:T(8,128)(2,1)} %top_tiles.1, ...), custom_call_target="tpu_custom_call" | custom-call | tf_op jit(solution)/shard_map/pallas_call | solution.py:463
  51.1 0.7 %copy.14 = bf16[1,3,256,256]{3,2,1,0:T(8,128)(2,1)} copy(bf16[1,3,256,256]{3,2,1,0:T(8,128)(2,1)S(1)} %get-tuple-element.2) | data formatting | bytes 786432
  51.8 0.7 %copy.15 = bf16[2,256,256]{2,1,0:T(8,128)(2,1)} copy(bf16[2,256,256]{2,1,0:T(8,128)(2,1)S(1)} %get-tuple-element.3) | data formatting | bytes 524288

commit v3 on v2

--- a/solution.py
+++ b/solution.py
@@ -214,21 +214,24 @@
         send_tiles(slot)
     for t in range(1, T):
         turn_rhs(t)
-    for copy in ld_cross:
-        copy.wait()
-    for a in range(A):
+    def prepare_cross():
+        for copy in ld_cross:
+            copy.wait()
         for t in range(T):
-            mask(cross_m, (a, t), cross_pat, (0, a, t))
-            send_tiles(LP + a * T + t)
-    for copy in ld_top:
-        copy.wait()
-    for slot in range(AP):
-        mask(top_m, (slot,), top_pat, (slot,))
-        send_tiles(LP + A * T + slot)
-    ld_arhs.wait()
-    ld_ainv.wait()
-    for a in range(A):
-        arhs_t[a] = arhs_in[a].T.reshape(L, HL, B)
+            for a in range(A):
+                mask(cross_m, (a, t), cross_pat, (0, a, t))
+                send_tiles(LP + a * T + t)
+
+    def prepare_top():
+        for copy in ld_top:
+            copy.wait()
+        for slot in range(AP):
+            mask(top_m, (slot,), top_pat, (slot,))
+            send_tiles(LP + A * T + slot)
+        ld_arhs.wait()
+        ld_ainv.wait()
+        for a in range(A):
+            arhs_t[a] = arhs_in[a].T.reshape(L, HL, B)
 
     def product(vectors, tiles, form=NT):
         return loop(
@@ -277,14 +280,36 @@
             ybuf[t, q, row] = solve(inv, t, residual, False).astype(BF16)
             send_y(t, q)
         fold_leaf(t - 1)
+        if t == 1:
+            prepare_cross()
+        if t == T - 1:
+            prepare_top()
+            for s in range(t):
+                for a in range(A):
+                    fold_ancestor(s, a)
+
+    last = T - 1
+    for a in range(A):
+        need(LP + a * T + last)
+
+    def last_block(source, a):
+        term = dot(whole(ybuf, last, source), cross_m[a, last, source], NT)
+        csum[a] += term.reshape(L, HL, B)
+
+    for a in range(A):
+        last_block(row, a)
+
+    def last_arrival(k):
+        for q in range(Q):
+            y_copy(last, q, k, row_from(k)).wait_recv()
         for a in range(A):
-            fold_ancestor(t - 1, a)
-
-    last = T - 1
+            last_block(row_from(k), a)
+
+    each(1, R - 1, last_arrival)
     for q in range(Q):
-        each(1, R, lambda k: y_copy(last, q, k, row_from(k)).wait_recv())
+        y_copy(last, q, R - 1, row_from(R - 1)).wait_recv()
     for a in range(A):
-        fold_ancestor(last, a)
+        last_block(row_from(R - 1), a)
         zs[a] = csum[a].astype(BF16)
         each(1, L, lambda k: lrs_copy(a, k).start())
 
@@ -300,11 +325,15 @@
     for a in range(A):
         residual = arhs_t[a, layer] - layer_sum(a)
         for s in range(a):
-            if s == a - 1:
-                each(1, R, lambda k: z_copy(s, k, row_from(k)).wait_recv())
-            residual = residual - product(
-                lambda k: zbuf[s, k], lambda k: top_m[pair_index(a, s), k]
-            )
+
+            def add_block(k, total):
+                source = row_from(k)
+                if s == a - 1:
+                    z_copy(s, k, source).wait_recv()
+                return total - dot(zbuf[s, source], top_m[pair_index(a, s), source], NT)
+
+            residual = residual - dot(zbuf[s, row], top_m[pair_index(a, s), row], NT)
+            residual = loop(1, R, add_block, residual)
         zbuf[a, row] = solve(ainv, a, residual, False).astype(BF16)
         if a < A - 1:
             each(1, R, lambda k: z_copy(a, R - k, row).start())

time: 52.7 us -> 52.6 us (level)
  no operation moved by 1% of the time
where the time goes in v3:
time: 52.6 us; the launch traced here: 52.4 us
  Pallas kernels  50.3 us (96%)
  local copies, waits for them, and re-layouts  1.45 us (3%)
  between operations  0.64 us (1%)
    pallas_call x1, Pallas kernels, local(): pl.pallas_call(functools.partial(kernel, dims), out_shape=(vmem(leaf_rhs....  50.3 us
    unnamed x2, local copies, waits for them, and re-layouts  1.45 us

profile of v3, /device:TPU:0, one launch (start us, length us, event | category | flops | bytes accessed | tf_op | source)
XLA Modules:
  0.0 52.4 jit_solution(8147831210101080499)
XLA Ops:
  0.6 50.3 %shard_map.113 = (bf16[1,3,256,256]{3,2,1,0:T(8,128)(2,1)S(1)}, bf16[2,256,256]{2,1,0:T(8,128)(2,1)S(1)}) custom-call(f32[1,3,256,256]{3,2,1,0:T(8,128)} %leaf_rhs.1, f32[2,256,256]{2,1,0:T(8,128)} %anc_rhs.1, bf16[1,3,256,512]{3,2,1,0:T(8,128)(2,1)} %leaf_tiles.1, bf16[1,2,3,256,512]{4,3,2,1,0:T(8,128)(2,1)} %cross_tiles.1, bf16[1,256,512]{2,1,0:T(8,128)(2,1)} %top_tiles.1, ...), custom_call_target="tpu_custom_call" | custom-call | tf_op jit(solution)/shard_map/pallas_call | solution.py:492
  51.0 0.7 %copy.14 = bf16[1,3,256,256]{3,2,1,0:T(8,128)(2,1)} copy(bf16[1,3,256,256]{3,2,1,0:T(8,128)(2,1)S(1)} %get-tuple-element.2) | data formatting | bytes 786432
  51.7 0.7 %copy.15 = bf16[2,256,256]{2,1,0:T(8,128)(2,1)} copy(bf16[2,256,256]{2,1,0:T(8,128)(2,1)S(1)} %get-tuple-element.3) | data formatting | bytes 524288

commit v4 on v3

--- a/solution.py
+++ b/solution.py
@@ -460,7 +460,7 @@
     B = leaf_rhs.shape[2]
     H = leaf_rhs.shape[3] // C
     W = arrays[8].shape[-1]
-    Q = 2 if R <= 4 and L % 2 == 0 else 1
+    Q = 1
     HQ, HL = H // Q, H // L
     SB = B // W
     LP, AP = T * (T - 1) // 2, A * (A - 1) // 2

time: 52.6 us -> 54.4 us (1.034)
  Pallas kernels: 50.3 us -> 52.1 us
    pallas_call x1, Pallas kernels: 50.3 us -> 52.1 us  [local(): pl.pallas_call(functools.partial(kernel, dims), out_shape=(vmem(leaf_rhs....]
where the time goes in v4:
time: 54.4 us; the launch traced here: 54.2 us
  Pallas kernels  52.1 us (96%)
  local copies, waits for them, and re-layouts  1.45 us (3%)
  between operations  0.64 us (1%)
    pallas_call x1, Pallas kernels, local(): pl.pallas_call(functools.partial(kernel, dims), out_shape=(vmem(leaf_rhs....  52.1 us
    unnamed x2, local copies, waits for them, and re-layouts  1.45 us

profile of v4, /device:TPU:0, one launch (start us, length us, event | category | flops | bytes accessed | tf_op | source)
XLA Modules:
  0.0 54.2 jit_solution(6831664343564586832)
XLA Ops:
  0.6 52.1 %shard_map.113 = (bf16[1,3,256,256]{3,2,1,0:T(8,128)(2,1)S(1)}, bf16[2,256,256]{2,1,0:T(8,128)(2,1)S(1)}) custom-call(f32[1,3,256,256]{3,2,1,0:T(8,128)} %leaf_rhs.1, f32[2,256,256]{2,1,0:T(8,128)} %anc_rhs.1, bf16[1,3,256,512]{3,2,1,0:T(8,128)(2,1)} %leaf_tiles.1, bf16[1,2,3,256,512]{4,3,2,1,0:T(8,128)(2,1)} %cross_tiles.1, bf16[1,256,512]{2,1,0:T(8,128)(2,1)} %top_tiles.1, ...), custom_call_target="tpu_custom_call" | custom-call | tf_op jit(solution)/shard_map/pallas_call | solution.py:492
  52.8 0.7 %copy.14 = bf16[1,3,256,256]{3,2,1,0:T(8,128)(2,1)} copy(bf16[1,3,256,256]{3,2,1,0:T(8,128)(2,1)S(1)} %get-tuple-element.2) | data formatting | bytes 786432
  53.5 0.7 %copy.15 = bf16[2,256,256]{2,1,0:T(8,128)(2,1)} copy(bf16[2,256,256]{2,1,0:T(8,128)(2,1)S(1)} %get-tuple-element.3) | data formatting | bytes 524288

commit v5 on v3

--- a/solution.py
+++ b/solution.py
@@ -94,6 +94,13 @@
     my_cols = pl.ds(pl.multiple_of(col * H, H), H)
     ld_rhs = [load(leaf_rhs.at[0, 0, :, my_cols], rhs_in.at[0])]
     ld_inv = load(leaf_inv.at[0, :, pl.ds(row * SB, SB)], inv)
+    barrier = pltpu.get_barrier_semaphore()
+    for name, mine, size in (("row", row, R), ("layer", layer, L), ("col", col, C)):
+        for step in range(1, size):
+            pl.semaphore_signal(
+                barrier, inc=1, device_id={name: ahead(mine, step, size)}, device_id_type=MESH
+            )
+
     ld_leaf = [
         load(leaf_tiles.at[0, :, :, pl.ds(j * B, B)], leaf_m.at[:, col * RC + j])
         for j in range(RC)
@@ -110,13 +117,6 @@
     ]
     ld_arhs = load(anc_rhs.at[:, :, my_cols], arhs_in)
     ld_ainv = load(anc_inv.at[:, pl.ds(row * SB, SB)], ainv)
-
-    barrier = pltpu.get_barrier_semaphore()
-    for name, mine, size in (("row", row, R), ("layer", layer, L), ("col", col, C)):
-        for step in range(1, size):
-            pl.semaphore_signal(
-                barrier, inc=1, device_id={name: ahead(mine, step, size)}, device_id_type=MESH
-            )
 
     def remote(src, dst, ssem, rsem, name, target):
         return pltpu.make_async_remote_copy(
@@ -391,6 +391,18 @@
 
         each(0, R, one)
 
+    def fold_ancestors(t, source=None):
+        def one(k):
+            term = None
+            for a in range(A):
+                more = dot(xanc[a].reshape(H, B), cross_m[a, t, k], NN)
+                term = more if term is None else term + more
+            if source is not None:
+                term = term + dot(xbuf[source].reshape(H, B), leaf_m[pair_index(source, t), k], NN)
+            bsum[t, :, k] = term.reshape(Q, HQ, B)
+
+        each(0, R, one)
+
     def fold_cross(a, t):
         fold_back(t, xanc[a].reshape(H, B), lambda k: cross_m[a, t, k], a == A - 1)
 
@@ -414,11 +426,8 @@
     each(1, L, lambda k: lag_copy(0, k, behind(layer, k, L)).wait_recv())
     for q in range(Q):
         start_level(T - 1, q)
-    for t in range(T - 2, -1, -1):
-        for a in range(A - 1, -1, -1):
-            fold_cross(a, t)
-    for a in range(A):
-        emit(T + a, xanc[a].reshape(H, B))
+    if T > 1:
+        fold_ancestors(T - 2)
     for t in range(T - 1, -1, -1):
         for q in range(Q):
 
@@ -430,9 +439,16 @@
             xbuf[t, q] = solve(inv, t, residual, True).astype(BF16)
             if t > 0:
                 start_level(t - 1, q)
+        if t > 1:
+            fold_ancestors(t - 2, t)
+            for upper in range(t + 1, T):
+                fold_back(
+                    t - 2, xbuf[upper].reshape(H, B), lambda k: leaf_m[pair_index(upper, t - 2), k]
+                )
         emit(t, xbuf[t].reshape(H, B))
-        for lower in range(t - 1):
-            fold_back(lower, xbuf[t].reshape(H, B), lambda k: leaf_m[pair_index(t, lower), k])
+        if t == min(1, T - 1):
+            for a in range(A):
+                emit(T + a, xanc[a].reshape(H, B))
 
     for slot in range(LP + A * T + AP):
         for k in range(1, C):
@@ -451,6 +467,17 @@
         for k in range(1, C):
             out_copy(slot, k, col).wait_send()
             out_copy(slot, k, behind(col, k, C)).wait_recv()
+
+
+def write_out(leaf_in, anc_in, leaf_out, anc_out, sems):
+    copies = [
+        pltpu.make_async_copy(leaf_in, leaf_out, sems.at[0]),
+        pltpu.make_async_copy(anc_in, anc_out, sems.at[1]),
+    ]
+    for copy in copies:
+        copy.start()
+    for copy in copies:
+        copy.wait()
 
 
 def local(R, L, C, *arrays):
@@ -489,7 +516,7 @@
     ]
     anywhere = pl.BlockSpec(memory_space=pl.ANY)
     scalars = pl.BlockSpec(memory_space=pltpu.SMEM)
-    return pl.pallas_call(
+    solved = pl.pallas_call(
         functools.partial(kernel, dims),
         out_shape=(
             vmem(leaf_rhs.shape, BF16),
@@ -502,6 +529,16 @@
             collective_id=0, has_side_effects=True, vmem_limit_bytes=56 * 1024 * 1024
         ),
     )(*arrays)
+    return pl.pallas_call(
+        write_out,
+        out_shape=(
+            jax.ShapeDtypeStruct(leaf_rhs.shape, BF16),
+            jax.ShapeDtypeStruct(anc_rhs.shape, BF16),
+        ),
+        in_specs=[pl.BlockSpec(memory_space=vmem)] * 2,
+        out_specs=(anywhere, anywhere),
+        scratch_shapes=[dma((2,))],
+    )(*solved)
 
 
 def solution(mesh):

time: 52.6 us -> 54.5 us (1.036)
  Pallas kernels: 50.3 us -> 52.2 us
    pallas_call x0 -> x1, Pallas kernels: none -> 1.92 us  [local(): pl.pallas_call(write_out, out_shape=(jax.ShapeDtypeStruct(leaf_rhs.shape,...]
    unnamed x2 -> x4, local copies, waits for them, and re-layouts: 1.45 us -> 1.45 us
where the time goes in v5:
time: 54.5 us; the launch traced here: 54.3 us
  Pallas kernels  52.2 us (96%)
  local copies, waits for them, and re-layouts  1.45 us (3%)
  between operations  0.65 us (1%)
    pallas_call x1, Pallas kernels, local(): pl.pallas_call(functools.partial(kernel, dims), out_shape=(vmem(leaf_rhs....  50.3 us
    pallas_call x1, Pallas kernels, local(): pl.pallas_call(write_out, out_shape=(jax.ShapeDtypeStruct(leaf_rhs.shape,...  1.92 us
    unnamed x4, local copies, waits for them, and re-layouts  1.45 us

profile of v5, /device:TPU:0, one launch (start us, length us, event | category | flops | bytes accessed | tf_op | source)
XLA Modules:
  0.0 54.3 jit_solution(5615612099056753677)
XLA Ops:
  0.6 50.3 %shard_map.113 = (bf16[1,3,256,256]{3,2,1,0:T(8,128)(2,1)S(1)}, bf16[2,256,256]{2,1,0:T(8,128)(2,1)S(1)}) custom-call(f32[1,3,256,256]{3,2,1,0:T(8,128)} %leaf_rhs.1, f32[2,256,256]{2,1,0:T(8,128)} %anc_rhs.1, bf16[1,3,256,512]{3,2,1,0:T(8,128)(2,1)} %leaf_tiles.1, bf16[1,2,3,256,512]{4,3,2,1,0:T(8,128)(2,1)} %cross_tiles.1, bf16[1,256,512]{2,1,0:T(8,128)(2,1)} %top_tiles.1, ...), custom_call_target="tpu_custom_call" | custom-call | tf_op jit(solution)/shard_map/pallas_call | solution.py:519
  50.9 0.0 copy-start
  50.9 0.7 %copy-done = bf16[1,3,256,256]{3,2,1,0:T(8,128)(2,1)} copy-done((bf16[1,3,256,256]{3,2,1,0:T(8,128)(2,1)}, bf16[1,3,256,256]{3,2,1,0:T(8,128)(2,1)S(1)}, u32[]{:S(2)}) %copy-start) | copy-done | bytes 393240
  51.7 0.0 copy-start.1
  51.7 0.7 %copy-done.1 = bf16[2,256,256]{2,1,0:T(8,128)(2,1)} copy-done((bf16[2,256,256]{2,1,0:T(8,128)(2,1)}, bf16[2,256,256]{2,1,0:T(8,128)(2,1)S(1)}, u32[]{:S(2)}) %copy-start.1) | copy-done | bytes 262168
  52.4 1.9 %shard_map.114 = (bf16[1,3,256,256]{3,2,1,0:T(8,128)(2,1)}, bf16[2,256,256]{2,1,0:T(8,128)(2,1)}) custom-call(bf16[1,3,256,256]{3,2,1,0:T(8,128)(2,1)} %copy-done, bf16[2,256,256]{2,1,0:T(8,128)(2,1)} %copy-done.1), custom_call_target="tpu_custom_call" | custom-call | tf_op jit(solution)/shard_map/pallas_call | solution.py:532
Async XLA Ops:
  50.9 0.8 %copy-start = (bf16[1,3,256,256]{3,2,1,0:T(8,128)(2,1)}, bf16[1,3,256,256]{3,2,1,0:T(8,128)(2,1)S(1)}, u32[]{:S(2)}) copy-start(bf16[1,3,256,256]{3,2,1,0:T(8,128)(2,1)S(1)} %get-tuple-element.4.leaf_in) | copy-start | bytes 1179652
  51.7 0.7 %copy-start.1 = (bf16[2,256,256]{2,1,0:T(8,128)(2,1)}, bf16[2,256,256]{2,1,0:T(8,128)(2,1)S(1)}, u32[]{:S(2)}) copy-start(bf16[2,256,256]{2,1,0:T(8,128)(2,1)S(1)} %get-tuple-element.5.anc_in) | copy-start | bytes 786436
